TPU v7x, 256 devices: a whole 4x4x8 slice. The times are simulated.
256 devices in a mesh: blk: 16 (over x, y_lo, core), en: 16 (over y_hi, z).
Axes of the slice: x: 4, y: 4 (y_hi: 2, y_lo: 2; y = y_hi * 2 + y_lo), z: 8, core: 2. Of those that a mesh axis runs over, the one named last changes fastest.
Arguments:
- panel: bfloat16 [64, 8192, 1024], P('en', 'blk'), may hold values from -0.26367188 to 0.26367188
- gamma: bfloat16 [64, 2, 512, 512], P('en'), may hold values from -1 to 3, as said below
- energy_point: int32 [64], P('en'), may hold values from 0 to 63, each once
Outputs:
- density: float32 [8192, 4, 512], P(('blk', 'en'))
Inputs may be any that keep to these rules, and one draw needn't show every extreme that they name: For each energy, gamma holds the real part (symmetric) and the imaginary part (antisymmetric) of a Hermitian matrix. `energy_point`: each grid point appears once.
All inputs are finite; a program needn't handle non-finite values.
Results may differ from a plain program's by a relative error of at most 0.00053.
Values may be sent and summed in bfloat16 or wider, within the bound.
A program may use at most 128 MiB of HBM per device.

v0:
```python
import jax
import jax.numpy as jnp
from jax import lax
from jax.sharding import PartitionSpec as P

ROUNDS = 3


THERMAL_LEVEL = 0.1


def from_partner(block, axis, distance):
    count = lax.axis_size(axis)
    route = []
    for low in range(count):
        high = low | 1 << distance
        if high != low and high < count:
            route += [(low, high), (high, low)]
    return lax.ppermute(block, axis, route)


def window_weight(energy_point, energies):
    energy_grid = (energy_point.astype(jnp.float32) + 0.5) / energies - 0.5
    upper_block = jax.nn.sigmoid((0.5 - energy_grid) / THERMAL_LEVEL)
    lower_block = jax.nn.sigmoid((-0.5 - energy_grid) / THERMAL_LEVEL)
    return (upper_block - lower_block) / energies


def block_form(gamma_one):
    real_part = gamma_one[0]
    imaginary_piece = gamma_one[1]
    upper_rows = jnp.concatenate([real_part, imaginary_piece], axis=1)
    lower_rows = jnp.concatenate([-imaginary_piece, real_part], axis=1)
    return jnp.concatenate([upper_rows, lower_rows], axis=0)


def local(panel, gamma, energy_point):
    energies = energy_point.shape[0] * lax.axis_size("en")
    fermi_weight = window_weight(energy_point, energies)
    forms = jax.vmap(block_form)(gamma)
    product = jnp.einsum("era,eab->erb", panel, forms, preferred_element_type=jnp.float32)
    mixed = (fermi_weight[:, None, None] * product).astype(jnp.bfloat16)

    def fetch_partner(level):
        return from_partner(panel, "blk", level)

    stacked = jnp.stack([panel] + [fetch_partner(level) for level in range(ROUNDS)], axis=1)
    return lax.psum_scatter(
        jnp.einsum("era,esca->rsc", mixed, stacked, preferred_element_type=jnp.float32),
        "en",
        scatter_dimension=0,
        tiled=True,
    )


def solution(mesh):
    in_specs = (P("en", "blk", None), P("en", None, None, None), P("en"))
    out_specs = P(("blk", "en"), None, None)
    return jax.shard_map(local, mesh=mesh, in_specs=in_specs, out_specs=out_specs, check_vma=False)
```

profile of v0, /device:TPU:2, one launch (start us, length us, event | category | flops | bytes accessed | tf_op | source)
XLA Modules:
  0.0 334.4 jit_solution(41742584681736861)
XLA Ops:
  6.5 0.0 reduce-scatter.2.cloned.1.call-start
  6.5 0.0 copy-start
  6.5 0.0 collective-permute-start
  6.5 2.3 collective-permute-start.2
  8.8 0.0 collective-permute-start.1
  8.8 0.7 fusion.28
  9.5 1.7 fusion.31
  11.2 0.0 copy-done
  11.2 0.0 copy-start.1
  11.2 0.3 slice_bitcast_fusion
  11.5 1.9 copy-done.1
  13.4 6.1 %fusion.47 = bf16[4,512,1024,1]{2,1,0,3:T(8,128)(2,1)} fusion(f32[4]{0:T(128)S(1)} %fusion.28, bf16[4,512,1024]{2,1,0:T(8,128)(2,1)S(1)} %copy-done.1, bf16[4,512,512]{2,1,0:T(8,128)(2,1)S(1)} %get-tuple-element.6, bf16[4,512,512]{2,1,0:T(8,128)(2,1)S(1)} %fusion.31, bf16[4,512,512]{2,1,0:T(8,128)(2,1)S(1)} %get-tuple-element.5), kind=kOutput, calls=%fused_computation.17.clone.clone.clone.clone.2 | convolution fusion | flops 4332716032 | bytes 14680080 | tf_op jit(solution)/shard_map/era,eab->erb/dot_general | solution.py:41
  19.5 0.0 collective-permute-done
  19.6 80.7 %collective-permute-done.2 = bf16[4,512,1024]{2,1,0:T(8,128)(2,1)S(1)} collective-permute-done((bf16[4,512,1024]{2,1,0:T(8,128)(2,1)}, bf16[4,512,1024]{2,1,0:T(8,128)(2,1)S(1)}, u32[]{:S(2)}, u32[]{:S(2)}) %collective-permute-start.2) | collective-permute-done | bytes 4194336 | tf_op jit(solution)/shard_map/ppermute | solution.py:19
  100.3 1.6 collective-permute-done.1
  101.8 13.3 %fusion.19 = f32[512,4,512]{2,0,1:T(8,128)} fusion(bf16[4,1,512,1024]{3,2,0,1:T(8,128)(2,1)S(1)} %bitcast.36, bf16[4,1,512,1024]{3,2,0,1:T(8,128)(2,1)} %bitcast.6, bf16[4,1,512,1024]{3,2,0,1:T(8,128)(2,1)S(1)} %bitcast.35, bf16[4,1,512,1024]{3,2,0,1:T(8,128)(2,1)S(1)} %bitcast.34, bf16[4,512,1024,1]{2,1,0,3:T(8,128)(2,1)} %fusion.47), kind=kOutput, calls=%fused_computation.19 | convolution fusion | flops 8657043456 | bytes 25165824 | tf_op jit(solution)/shard_map/era,esca->rsc/dot_general | solution.py:49
  115.1 0.0 reduce-scatter.2.cloned.1.call-update
  115.2 210.6 %reduce-scatter.2.cloned.1.call-done = f32[32,4,512]{2,0,1:T(8,128)} async-done(((f32[512,4,512]{2,0,1:T(8,128)}), f32[32,4,512]{2,0,1:T(8,128)}) %reduce-scatter.2.cloned.1.call-update) | async-done | bytes 262160 | tf_op jit(solution)/shard_map/reduce_scatter | solution.py:48
  325.7 1.8 copy.5
Async XLA Ops:
  6.5 319.2 %reduce-scatter.2.cloned.1.call-start = ((), (), s32[]{:S(2)}) async-start(), calls=%async_computation.1 | async-start | bytes 4456448 | tf_op jit(solution)/shard_map/reduce_scatter | solution.py:48
  6.5 4.7 %copy-start = (bf16[4,2,512,512]{3,2,1,0:T(8,128)(2,1)S(1)}, bf16[4,2,512,512]{3,2,1,0:T(8,128)(2,1)}, u32[]{:S(2)}) copy-start(bf16[4,2,512,512]{3,2,1,0:T(8,128)(2,1)} %param.4) | copy-start | bytes 12582916
  6.5 13.0 %collective-permute-start = (bf16[4,512,1024]{2,1,0:T(8,128)(2,1)}, bf16[4,512,1024]{2,1,0:T(8,128)(2,1)S(1)}, u32[]{:S(2)}, u32[]{:S(2)}) collective-permute-start(bf16[4,512,1024]{2,1,0:T(8,128)(2,1)} %param.3), channel_id=1, source_target_pairs={{0,16},{16,0},{32,48},{48,32},{64,80},{80,64},{96,112},{112,96},{1... | collective-permute-start | bytes 12582920 | tf_op jit(solution)/shard_map/ppermute | solution.py:19
  6.5 93.7 %collective-permute-start.2 = (bf16[4,512,1024]{2,1,0:T(8,128)(2,1)}, bf16[4,512,1024]{2,1,0:T(8,128)(2,1)S(1)}, u32[]{:S(2)}, u32[]{:S(2)}) collective-permute-start(bf16[4,512,1024]{2,1,0:T(8,128)(2,1)} %param.3), channel_id=1, source_target_pairs={{0,64},{64,0},{16,80},{80,16},{32,96},{96,32},{48,112},{112,48},{1... | collective-permute-start | bytes 12582920 | tf_op jit(solution)/shard_map/ppermute | solution.py:19
  8.8 93.0 %collective-permute-start.1 = (bf16[4,512,1024]{2,1,0:T(8,128)(2,1)}, bf16[4,512,1024]{2,1,0:T(8,128)(2,1)}, u32[]{:S(2)}, u32[]{:S(2)}) collective-permute-start(bf16[4,512,1024]{2,1,0:T(8,128)(2,1)} %param.3), channel_id=1, source_target_pairs={{0,32},{32,0},{16,48},{48,16},{64,96},{96,64},{80,112},{112,80},{1... | collective-permute-start | bytes 12582920 | tf_op jit(solution)/shard_map/ppermute | solution.py:19
  11.2 2.2 copy-start.1
Sparse Core Ops, SparseCore 0:
  115.3 210.3 reduce-scatter.1
where the time goes:
time: 335 us; the launch traced here: 334 us
  waiting for transfers between devices  293 us (87%)
  matrix products  19.4 us (6%)
  between operations  13.4 us (4%)
  local copies, waits for them, and re-layouts  4 us (1%)
    reduce_scatter x1, waiting for transfers between devices, local(): lax.psum_scatter(jnp.einsum('era,esca->rsc', mixed, stacked, preferred_el...  211 us
    ppermute x3, waiting for transfers between devices, from_partner(): return lax.ppermute(block, axis, route)  82.3 us
    dot_general x1, matrix products, local(): jnp.einsum('era,esca->rsc', mixed, stacked, preferred_element_type=jnp.fl...  13.3 us
  transfers between devices with their start and end apart: 4, of which 3 were waited for; matrix products, arithmetic and copies ran while one was open for 3% of the time, Pallas kernels for 0%

commit v1 on v0

v1 whole, which is shorter than its diff:
```python
import functools

import jax
import jax.numpy as jnp
from jax import lax
from jax.experimental import pallas as pl
from jax.experimental.pallas import tpu as pltpu
from jax.sharding import PartitionSpec as P

THERMAL_LEVEL = 0.1
ENERGIES = 64
Z = 8
MESH = pl.DeviceIdType.MESH
F32 = jnp.float32
BF16 = jnp.bfloat16


def window_weight(energy_point, shape):
    grid = (jnp.full(shape, energy_point.astype(F32)) + 0.5) / ENERGIES - 0.5
    upper = jax.nn.sigmoid((0.5 - grid) / THERMAL_LEVEL)
    lower = jax.nn.sigmoid((-0.5 - grid) / THERMAL_LEVEL)
    return (upper - lower) / ENERGIES


def dot(a, b):
    return jnp.dot(a, b, preferred_element_type=F32)


def dot_nt(a, b):
    return lax.dot_general(a, b, (((1,), (1,)), ((), ())), preferred_element_type=F32)


def interleave(first, second):
    group = lax.broadcasted_iota(jnp.int32, (32, 128), 1) // 16
    halves = []
    for low in (0, 4):
        total = jnp.zeros((32, 128), F32)
        for at in range(8):
            source = first if at % 2 == 0 else second
            shift = (16 * (at - at // 2 - low)) % 128
            moved = pltpu.roll(source, shift, 1) if shift else source
            total = jnp.where(group == at, moved, total)
        halves.append(total)
    return jnp.concatenate(halves, axis=1)


def kernel(energy, panel, panel_rows, gamma, out,
           own, near, far, broad, mixed, part, ring, give, got, q_part, q_got, t_part, t_got,
           own_sem, broad_sem, near_sem, far_send, far_recv, ring_send, ring_recv,
           give_sem, q_send, q_recv, t_send, t_recv):
    b, k = lax.axis_index("blk"), lax.axis_index("en")
    core, y_lo, x_lo = b % 2, (b // 2) % 2, (b // 4) % 2
    y_hi, z = k // Z, k % Z
    parity = (core + y_lo + x_lo) % 2
    core_mate = b + 1 - 2 * core
    y_mate = b + 2 - 4 * y_lo
    x_mate = b + 4 - 8 * x_lo
    to = parity * x_mate + (1 - parity) * y_mate
    source = parity * y_mate + (1 - parity) * x_mate
    k_mate = k + Z - 2 * Z * y_hi
    sign = 1 - 2 * core
    ahead = y_hi * Z + (z + sign + Z) % Z
    behind = y_hi * Z + (z - sign + Z) % Z

    loads = []
    for e in range(4):
        loads.append((pltpu.make_async_copy(panel.at[e], own.at[e], own_sem.at[e]),
                      pltpu.make_async_copy(gamma.at[e], broad.at[e], broad_sem.at[e])))
        for load in loads[-1]:
            load.start()

    barrier = pltpu.get_barrier_semaphore()
    peers = [(b, ahead), (b, behind), (core_mate, k), (y_mate, k), (x_mate, k),
             (b, k_mate), (y_mate, k_mate), (x_mate, k_mate)]
    for peer in peers:
        pl.semaphore_signal(barrier, inc=1, device_id=peer, device_id_type=MESH)
    pl.semaphore_wait(barrier, len(peers))

    def remote(src, dst, send, recv, device):
        return pltpu.make_async_remote_copy(src_ref=src, dst_ref=dst, send_sem=send, recv_sem=recv,
                                            device_id=device, device_id_type=MESH)

    sent = []

    def send(copy):
        copy.start()
        sent.append(copy)

    far_copies = [remote(panel_rows.at[:, c // 2, :, c % 2], far.at[c], far_send.at[c], far_recv.at[c], (to, k))
                  for c in range(4)]
    for copy in far_copies:
        send(copy)
    near_copy = remote(panel, near, near_sem.at[0], near_sem.at[1], (core_mate, k))
    send(near_copy)

    for e in range(4):
        for load in loads[e]:
            load.wait()
        weight = window_weight(energy[e], (1, 256))

        def columns(n, carry, e=e, weight=weight):
            at = pl.ds(pl.multiple_of(n * 256, 256), 256)
            real, imaginary = own[e, :, :512], own[e, :, 512:]
            gamma_real, gamma_imaginary = broad[e, 0, :, at], broad[e, 1, :, at]
            mixed[e, :, at] = (weight * (dot(real, gamma_real) - dot(imaginary, gamma_imaginary))).astype(BF16)
            mixed[e, :, pl.ds(pl.multiple_of(512 + n * 256, 256), 256)] = (
                weight * (dot(real, gamma_imaginary) + dot(imaginary, gamma_real))).astype(BF16)
            return carry

        lax.fori_loop(0, 2, columns, 0)

    def ring_copy(u, step):
        first = step in (0, 4)
        if step < 4:
            device, src = (b, ahead), part.at[u, (z + 4 * sign + Z) % Z] if first else ring.at[u, step - 1]
        else:
            device, src = (b, behind), part.at[u, (z - 3 * sign + Z) % Z] if first else ring.at[u, step - 1]
        return remote(src, ring.at[u, step], ring_send.at[u, step], ring_recv.at[u, step], device)

    def ring_first(u):
        send(ring_copy(u, 0))
        send(ring_copy(u, 4))

    def ring_next(u, step):
        ring_copy(u, step - 1).wait_recv()
        ring[u, step - 1] += part[u, (z + (4 - step) * sign + Z) % Z]
        send(ring_copy(u, step))
        if step < 3:
            ring_copy(u, step + 3).wait_recv()
            ring[u, step + 3] += part[u, (z - (3 - step) * sign + Z) % Z]
            send(ring_copy(u, step + 4))

    def ring_wait(u):
        ring_copy(u, 3).wait_recv()
        ring_copy(u, 6).wait_recv()

    def ring_total(u):
        return part[u, z] + ring[u, 3] + ring[u, 6]

    def whole_block(slot, rows):
        def columns(n, carry):
            at = pl.ds(pl.multiple_of(n * 256, 256), 256)
            total = dot_nt(mixed[0], rows[0, at, :])
            for e in range(1, 4):
                total += dot_nt(mixed[e], rows[e, at, :])
            part[2 * slot, :, :, at] = total[:256].reshape(8, 32, 256)
            part[2 * slot + 1, :, :, at] = total[256:].reshape(8, 32, 256)
            return carry

        lax.fori_loop(0, 2, columns, 0)
        ring_first(2 * slot)
        ring_first(2 * slot + 1)

    def give_copy(slot):
        return remote(give.at[slot], got.at[slot], give_sem.at[slot, 0], give_sem.at[slot, 1], (b, k_mate))

    def whole_end(slot):
        ring_wait(2 * slot)
        ring_wait(2 * slot + 1)
        give[slot] = ring_total(2 * slot + 1 - y_hi)
        send(give_copy(slot))
        out[slot] = ring_total(2 * slot + y_hi)

    def chunk_block(c):
        far_copies[c].wait_recv()

        def columns(n, carry):
            at = pl.ds(pl.multiple_of(n * 256, 256), 256)
            total = dot_nt(far[c, 0].reshape(128, 1024), mixed[0, at, :])
            for e in range(1, 4):
                total += dot_nt(far[c, e].reshape(128, 1024), mixed[e, at, :])
            part[4 + c, :, 0:16, at] = total.reshape(8, 16, 256)
            turned = total.T.reshape(8, 2, 16, 128)
            for low in range(2):
                part[4 + c, :, 16:32, pl.ds(pl.multiple_of(n * 256 + low * 128, 128), 128)] = turned[:, low]
            return carry

        lax.fori_loop(0, 2, columns, 0)
        ring_first(4 + c)

    def q_copy(c):
        return remote(q_part.at[c, 1 - y_hi], q_got.at[c], q_send.at[c], q_recv.at[c], (b, k_mate))

    def t_copy(c, from_y):
        return remote(t_part.at[c], t_got.at[c % 2, from_y], t_send.at[c], t_recv.at[c % 2, from_y],
                      (source, (c // 2) * Z + z))

    def chunk_end(c):
        ring_wait(4 + c)
        total = ring_total(4 + c)
        t_part[c] = total[:16]
        send(t_copy(c, y_hi))
        q_part[c, 0] = total[16:, :256]
        q_part[c, 1] = total[16:, 256:]
        send(q_copy(c))

    whole_block(0, own)
    near_copy.wait_recv()
    whole_block(1, near)
    for u in range(4):
        ring_next(u, 1)
    chunk_block(0)
    for u in range(4):
        ring_next(u, 2)
    ring_next(4, 1)
    for u in range(4):
        ring_next(u, 3)
    ring_next(4, 2)
    whole_end(0)
    whole_end(1)
    ring_next(4, 3)
    chunk_block(1)
    chunk_end(0)
    for step in (1, 2, 3):
        ring_next(5, step)
    chunk_end(1)
    chunk_block(2)
    for step in (1, 2, 3):
        ring_next(6, step)
    chunk_end(2)
    chunk_block(3)
    for step in (1, 2, 3):
        ring_next(7, step)
    chunk_end(3)

    for slot in range(2):
        give_copy(slot).wait_recv()
        out[slot] += got[slot]
    for c in range(4):
        q_copy(c).wait_recv()
    for h in range(2):
        pieces = []
        for c in (2 * h, 2 * h + 1):
            total = q_part[c, y_hi] + q_got[c]
            pieces.append(jnp.concatenate([total[:, :128], total[:, 128:]], axis=0))
        out[3 - parity, :, 256 * h:256 * h + 256] = interleave(*pieces)
    for half in range(2):
        for from_y in range(2):
            t_copy(half, from_y).wait_recv()
        out[2 + parity, 16 * half:16 * half + 16] = t_got[half, 0] + t_got[half, 1]
    for copy in sent:
        copy.wait_send()


def local(panel, gamma, energy_point):
    any_space = pl.BlockSpec(memory_space=pl.ANY)
    dma = pltpu.SemaphoreType.DMA
    blocks = pl.pallas_call(
        kernel,
        out_shape=jax.ShapeDtypeStruct((4, 32, 512), F32),
        in_specs=[pl.BlockSpec(memory_space=pltpu.SMEM), any_space, any_space, any_space],
        out_specs=pl.BlockSpec(memory_space=pltpu.VMEM),
        scratch_shapes=[
            pltpu.VMEM((4, 512, 1024), BF16),
            pltpu.VMEM((4, 512, 1024), BF16),
            pltpu.VMEM((4, 4, 8, 16, 1024), BF16),
            pltpu.VMEM((4, 2, 512, 512), BF16),
            pltpu.VMEM((4, 512, 1024), BF16),
            pltpu.VMEM((8, 8, 32, 512), F32),
            pltpu.VMEM((8, 7, 32, 512), F32),
            pltpu.VMEM((2, 32, 512), F32),
            pltpu.VMEM((2, 32, 512), F32),
            pltpu.VMEM((4, 2, 16, 256), F32),
            pltpu.VMEM((4, 16, 256), F32),
            pltpu.VMEM((4, 16, 512), F32),
            pltpu.VMEM((2, 2, 16, 512), F32),
            dma((4,)), dma((4,)), dma((2,)), dma((4,)), dma((4,)), dma((8, 7)), dma((8, 7)),
            dma((2, 2)), dma((4,)), dma((4,)), dma((4,)), dma((2, 2)),
        ],
        compiler_params=pltpu.CompilerParams(collective_id=0, has_side_effects=True, vmem_limit_bytes=56 * 2**20),
        cost_estimate=pl.CostEstimate(flops=13_000_000_000, bytes_accessed=12 * 2**20, transcendentals=0),
        name="density",
    )(energy_point, panel, panel.reshape(4, 2, 8, 2, 16, 1024), gamma)
    return jnp.transpose(blocks, (1, 0, 2))


def solution(mesh):
    in_specs = (P("en", "blk", None), P("en", None, None, None), P("en"))
    out_specs = P(("blk", "en"), None, None)
    return jax.shard_map(local, mesh=mesh, in_specs=in_specs, out_specs=out_specs, check_vma=False)
```

time: 335 us -> 98.4 us (0.29)
  waiting for transfers between devices: 293 us -> 0 us
  Pallas kernels: 0 us -> 96.4 us
  matrix products: 19.4 us -> 0 us
  between operations: 13.4 us -> 0.01 us
    reduce_scatter x1 -> x0, waiting for transfers between devices: 211 us -> none  [local(): lax.psum_scatter(jnp.einsum('era,esca->rsc', mixed, stacked, preferred_el...]
    pallas_call x0 -> x1, Pallas kernels: none -> 96.4 us  [local(): pl.pallas_call(kernel, out_shape=jax.ShapeDtypeStruct((4, 32, 512), F32),...]
    ppermute x3 -> x0, waiting for transfers between devices: 82.3 us -> none  [from_partner(): return lax.ppermute(block, axis, route)]
    dot_general x2 -> x0, matrix products: 19.4 us -> none  [the longest x1 13.3 us: local(): jnp.einsum('era,esca->rsc', mixed, stacked, preferred_element_type=jnp.fl...]
  transfers between devices with their start and end apart: 4 -> 0, of which waited for: 3 -> 0; matrix products, arithmetic and copies ran while one was open for 3% -> 0% of each run, Pallas kernels for 0% -> 0%
where the time goes in v1:
time: 98.4 us; the launch traced here: 98.3 us
  Pallas kernels  96.4 us (98%)
  local copies, waits for them, and re-layouts  1.82 us (2%)
    pallas_call x1, Pallas kernels, local(): pl.pallas_call(kernel, out_shape=jax.ShapeDtypeStruct((4, 32, 512), F32),...  96.4 us

profile of v1, /device:TPU:2, one launch (start us, length us, event | category | flops | bytes accessed | tf_op | source)
XLA Modules:
  0.0 98.3 jit_solution(9194076177628913247)
XLA Ops:
  0.0 96.4 %density.1 = f32[4,32,512]{2,1,0:T(8,128)} custom-call(s32[4]{0:T(128)} %energy.1, bf16[4,512,1024]{2,1,0:T(8,128)(2,1)} %panel.1, bf16[4,2,8,2,16,1024]{5,4,3,2,1,0:T(8,128)(2,1)} %bitcast.3, bf16[4,2,512,512]{3,2,1,0:T(8,128)(2,1)} %gamma.1), custom_call_target="tpu_custom_call" | custom-call | flops 12999999488 | bytes 12582912 | tf_op jit(solution)/shard_map/density/pallas_call | solution.py:248
  96.4 1.8 %copy.4 = f32[32,4,512]{2,1,0:T(4,128)} copy(f32[32,4,512]{2,0,1:T(8,128)} %bitcast.2) | data formatting | bytes 524288 | tf_op jit(solution)/shard_map/transpose | solution.py:274

commit v2 on v1

--- a/solution.py
+++ b/solution.py
@@ -45,8 +45,8 @@
 
 
 def kernel(energy, panel, panel_rows, gamma, out,
-           own, near, far, broad, mixed, part, ring, give, got, q_part, q_got, t_part, t_got,
-           own_sem, broad_sem, near_sem, far_send, far_recv, ring_send, ring_recv,
+           own, near, far, broad, mixed, part, ring, piece, piece_got, give, got, q_part, q_got, t_part, t_got,
+           own_sem, broad_sem, near_sem, far_send, far_recv, ring_send, ring_recv, piece_send, piece_recv,
            give_sem, q_send, q_recv, t_send, t_recv):
     b, k = lax.axis_index("blk"), lax.axis_index("en")
     core, y_lo, x_lo = b % 2, (b // 2) % 2, (b // 4) % 2
@@ -70,8 +70,9 @@
             load.start()
 
     barrier = pltpu.get_barrier_semaphore()
-    peers = [(b, ahead), (b, behind), (core_mate, k), (y_mate, k), (x_mate, k),
-             (b, k_mate), (y_mate, k_mate), (x_mate, k_mate)]
+    peers = [(b, y_hi * Z + (z + d) % Z) for d in range(1, Z)] + [
+        (core_mate, k), (y_mate, k), (x_mate, k),
+        (b, k_mate), (y_mate, k_mate), (x_mate, k_mate)]
     for peer in peers:
         pl.semaphore_signal(barrier, inc=1, device_id=peer, device_id_type=MESH)
     pl.semaphore_wait(barrier, len(peers))
@@ -161,6 +162,10 @@
         send(give_copy(slot))
         out[slot] = ring_total(2 * slot + y_hi)
 
+    def piece_copy(c, d):
+        return remote(piece.at[c, (z + d) % Z], piece_got.at[c, d - 1], piece_send.at[c, d - 1], piece_recv.at[c, d - 1],
+                      (b, y_hi * Z + (z + d) % Z))
+
     def chunk_block(c):
         far_copies[c].wait_recv()
 
@@ -169,14 +174,19 @@
             total = dot_nt(far[c, 0].reshape(128, 1024), mixed[0, at, :])
             for e in range(1, 4):
                 total += dot_nt(far[c, e].reshape(128, 1024), mixed[e, at, :])
-            part[4 + c, :, 0:16, at] = total.reshape(8, 16, 256)
+            rows = total.reshape(8, 16, 256)
+            part[4 + c, :, 0:16, at] = rows
+            piece[c, :, 0:16, at] = rows.astype(BF16)
             turned = total.T.reshape(8, 2, 16, 128)
             for low in range(2):
-                part[4 + c, :, 16:32, pl.ds(pl.multiple_of(n * 256 + low * 128, 128), 128)] = turned[:, low]
+                lanes = pl.ds(pl.multiple_of(n * 256 + low * 128, 128), 128)
+                part[4 + c, :, 16:32, lanes] = turned[:, low]
+                piece[c, :, 16:32, lanes] = turned[:, low].astype(BF16)
             return carry
 
         lax.fori_loop(0, 2, columns, 0)
-        ring_first(4 + c)
+        for d in (4, 3, 5, 2, 6, 1, 7):
+            send(piece_copy(c, d))
 
     def q_copy(c):
         return remote(q_part.at[c, 1 - y_hi], q_got.at[c], q_send.at[c], q_recv.at[c], (b, k_mate))
@@ -186,8 +196,10 @@
                       (source, (c // 2) * Z + z))
 
     def chunk_end(c):
-        ring_wait(4 + c)
-        total = ring_total(4 + c)
+        total = part[4 + c, z]
+        for d in (1, 7, 2, 6, 3, 5, 4):
+            piece_copy(c, d).wait_recv()
+            total += piece_got[c, d - 1].astype(F32)
         t_part[c] = total[:16]
         send(t_copy(c, y_hi))
         q_part[c, 0] = total[16:, :256]
@@ -197,30 +209,21 @@
     whole_block(0, own)
     near_copy.wait_recv()
     whole_block(1, near)
+    chunk_block(0)
     for u in range(4):
         ring_next(u, 1)
-    chunk_block(0)
     for u in range(4):
         ring_next(u, 2)
-    ring_next(4, 1)
+    chunk_block(1)
     for u in range(4):
         ring_next(u, 3)
-    ring_next(4, 2)
+    chunk_end(0)
     whole_end(0)
     whole_end(1)
-    ring_next(4, 3)
-    chunk_block(1)
-    chunk_end(0)
-    for step in (1, 2, 3):
-        ring_next(5, step)
+    chunk_block(2)
     chunk_end(1)
-    chunk_block(2)
-    for step in (1, 2, 3):
-        ring_next(6, step)
+    chunk_block(3)
     chunk_end(2)
-    chunk_block(3)
-    for step in (1, 2, 3):
-        ring_next(7, step)
     chunk_end(3)
 
     for slot in range(2):
@@ -257,14 +260,16 @@
             pltpu.VMEM((4, 2, 512, 512), BF16),
             pltpu.VMEM((4, 512, 1024), BF16),
             pltpu.VMEM((8, 8, 32, 512), F32),
-            pltpu.VMEM((8, 7, 32, 512), F32),
+            pltpu.VMEM((4, 7, 32, 512), F32),
+            pltpu.VMEM((4, 8, 32, 512), BF16),
+            pltpu.VMEM((4, 7, 32, 512), BF16),
             pltpu.VMEM((2, 32, 512), F32),
             pltpu.VMEM((2, 32, 512), F32),
             pltpu.VMEM((4, 2, 16, 256), F32),
             pltpu.VMEM((4, 16, 256), F32),
             pltpu.VMEM((4, 16, 512), F32),
             pltpu.VMEM((2, 2, 16, 512), F32),
-            dma((4,)), dma((4,)), dma((2,)), dma((4,)), dma((4,)), dma((8, 7)), dma((8, 7)),
+            dma((4,)), dma((4,)), dma((2,)), dma((4,)), dma((4,)), dma((4, 7)), dma((4, 7)), dma((4, 7)), dma((4, 7)),
             dma((2, 2)), dma((4,)), dma((4,)), dma((4,)), dma((2, 2)),
         ],
         compiler_params=pltpu.CompilerParams(collective_id=0, has_side_effects=True, vmem_limit_bytes=56 * 2**20),

time: 98.4 us -> 76.3 us (0.78); the launches traced: 98.3 us -> 75 us
  Pallas kernels: 96.4 us -> 73.2 us
    pallas_call x1, Pallas kernels: 96.4 us -> 73.2 us  [local(): pl.pallas_call(kernel, out_shape=jax.ShapeDtypeStruct((4, 32, 512), F32),...]
where the time goes in v2:
time: 76.3 us; the launch traced here: 75 us
  Pallas kernels  73.2 us (96%)
  local copies, waits for them, and re-layouts  1.82 us (2%)
    pallas_call x1, Pallas kernels, local(): pl.pallas_call(kernel, out_shape=jax.ShapeDtypeStruct((4, 32, 512), F32),...  73.2 us
    transpose x1, local copies, waits for them, and re-layouts, local(): return jnp.transpose(blocks, (1, 0, 2))  1.82 us

profile of v2, /device:TPU:2, one launch (start us, length us, event | category | flops | bytes accessed | tf_op | source)
XLA Modules:
  0.0 75.0 jit_solution(17261191931261237317)
XLA Ops:
  0.0 73.2 %density.1 = f32[4,32,512]{2,1,0:T(8,128)} custom-call(s32[4]{0:T(128)} %energy.1, bf16[4,512,1024]{2,1,0:T(8,128)(2,1)} %panel.1, bf16[4,2,8,2,16,1024]{5,4,3,2,1,0:T(8,128)(2,1)} %bitcast.3, bf16[4,2,512,512]{3,2,1,0:T(8,128)(2,1)} %gamma.1), custom_call_target="tpu_custom_call" | custom-call | flops 12999999488 | bytes 12582912 | tf_op jit(solution)/shard_map/density/pallas_call | solution.py:251
  73.2 1.8 %copy.4 = f32[32,4,512]{2,1,0:T(4,128)} copy(f32[32,4,512]{2,0,1:T(8,128)} %bitcast.2) | data formatting | bytes 524288 | tf_op jit(solution)/shard_map/transpose | solution.py:279
